TPU v7x, 128 devices: a whole 4x4x4 slice. The times are simulated.
128 devices in a mesh: ctx: 16 (over x_lo, z, core), tp: 8 (over y, x_hi).
Axes of the slice: x: 4 (x_hi: 2, x_lo: 2; x = x_hi * 2 + x_lo), y: 4, z: 4, core: 2. Of those that a mesh axis runs over, the one named last changes fastest.
Arguments:
- tokens: bfloat16 [16384, 1024], P(('ctx', 'tp')), may hold values from -6 to 6
- block_table: int32 [16, 2], replicated, may hold values from 0 to 31, as said below
- doc_ids: int32 [4, 4096], replicated, may hold values from 0 to 3, never falling along the last dimension, each value on 1 to 2048 neighbouring positions
- attn_gain: bfloat16 [1024], P('ctx'), may hold values from 0.25 to 1.75
- w_query: bfloat16 [1024, 2048], P('ctx', 'tp'), may hold values from -0.1875 to 0.1875
- w_key: bfloat16 [1024, 1024], P('ctx', 'tp'), may hold values from -0.1875 to 0.1875
- w_value: bfloat16 [1024, 1024], P('ctx', 'tp'), may hold values from -0.1875 to 0.1875
- query_gain: bfloat16 [128], P('ctx'), may hold values from 0.25 to 1.75
- key_gain: bfloat16 [128], P('ctx'), may hold values from 0.25 to 1.75
- w_out: bfloat16 [2048, 1024], P('tp', 'ctx'), may hold values from -1 to 1
- ffn_gain: bfloat16 [1024], P('ctx'), may hold values from 0.25 to 1.75
- w_gate: bfloat16 [1024, 3072], P('ctx', 'tp'), may hold values from -0.1875 to 0.1875
- w_up: bfloat16 [1024, 3072], P('ctx', 'tp'), may hold values from -0.1875 to 0.1875
- w_down: bfloat16 [3072, 1024], P('tp', 'ctx'), may hold values from -0.109375 to 0.109375
- out_grad: bfloat16 [16384, 1024], P(('ctx', 'tp')), may hold values from -6 to 6
Outputs:
- out: bfloat16 [16384, 1024], P(('ctx', 'tp'))
- grad_x: bfloat16 [16384, 1024], P(('ctx', 'tp'))
- grad_attn_gain: float32 [1024], P('ctx')
- grad_w_query: float32 [1024, 2048], P('ctx', 'tp')
- grad_w_key: float32 [1024, 1024], P('ctx', 'tp')
- grad_w_value: float32 [1024, 1024], P('ctx', 'tp')
- grad_query_gain: float32 [128], P('ctx')
- grad_key_gain: float32 [128], P('ctx')
- grad_w_out: float32 [2048, 1024], P('tp', 'ctx')
- grad_ffn_gain: float32 [1024], P('ctx')
- grad_w_gate: float32 [1024, 3072], P('ctx', 'tp')
- grad_w_up: float32 [1024, 3072], P('ctx', 'tp')
- grad_w_down: float32 [3072, 1024], P('tp', 'ctx')
Inputs may be any that keep to these rules, and one draw needn't show every extreme that they name: `block_table`: row c holds a block b below 16 and its mirror 2 * 16 - 1 - b; the first entries of the rows form a permutation, so every block appears once. `doc_ids`: never falling along a row; each document has 1 to 2048 positions, one exactly that many.
All inputs are finite; a program needn't handle non-finite values.
Results may differ from a plain program's by a relative error of at most 0.025.
Values may be sent and summed in bfloat16 or wider, within the bound.
No kernel may reach another device: no remote copies, remote signals or barrier semaphores. Data moves between devices by JAX's collectives and lax.ppermute only.
A program may use at most 192 MiB of HBM per device.

v0:
```python
import math
import jax
import jax.numpy as jnp
from jax import lax
from jax.sharding import PartitionSpec as P

HD = 128
EPS = 1e-06
THETA = 1000000.0
NEG_SCORE = -1e30


def split_up(shard, dim, length):
    before, after = (shard.shape[:dim], shard.shape[dim + 1 :])
    return jnp.moveaxis(shard.reshape(*before, length, -1, *after), dim, 0)


def sent_and_summed(shard, axis, dim):
    parts = split_up(shard, dim, lax.axis_size(axis))
    arrived = lax.all_to_all(parts, axis, split_axis=0, concat_axis=0, tiled=True)
    return arrived.astype(jnp.float32).sum(axis=0)


def normed(values, norm_gain):
    return values * lax.rsqrt(jnp.mean(values * values, axis=-1, keepdims=True) + EPS) * norm_gain


def rotate(values, cos_table, sin_table):
    half_width = values.shape[-1] // 2
    turned = jnp.concatenate([-values[..., half_width:], values[..., :half_width]], axis=-1)
    return values * cos_table + turned * sin_table


def contract_last(left_side, right_side):
    return lax.dot_general(
        left_side, right_side, (((1,), (1,)), ((), ())), preferred_element_type=jnp.float32
    )


def contract_first(left_side, right_side):
    return lax.dot_general(
        left_side, right_side, (((0,), (0,)), ((), ())), preferred_element_type=jnp.float32
    )


def send_grads(stacked):
    return lax.psum_scatter(
        stacked.astype(jnp.bfloat16), "ctx", scatter_dimension=0, tiled=True
    ).astype(jnp.float32)


def per_device(
    tokens,
    block_table,
    doc_ids,
    attn_gain,
    w_query,
    w_key,
    w_value,
    query_gain,
    key_gain,
    w_out,
    ffn_gain,
    w_gate,
    w_up,
    w_down,
    out_grad,
):
    ctx_count = lax.axis_size("ctx")
    tp_count = lax.axis_size("tp")
    ctx_rank = lax.axis_index("ctx")
    rows_dev = tokens.shape[0]
    local_rows = rows_dev * tp_count
    seq_count = doc_ids.shape[0]
    pair_rows = local_rows // seq_count
    seq_keys = pair_rows * ctx_count
    q_heads = w_query.shape[1] // HD
    kv_heads = w_key.shape[1] // HD
    group_size = q_heads // kv_heads
    q_width = q_heads * HD
    k_width = kv_heads * HD
    ff_local = w_gate.shape[1]
    score_scale = HD ** (-0.5)
    key_block = math.gcd(seq_keys, 512)
    key_blocks = seq_keys // key_block
    seq_len = doc_ids.shape[1]
    half_block = pair_rows // 2
    seq_index = jnp.arange(seq_len, dtype=jnp.int32)
    change = jnp.concatenate(
        [jnp.ones((seq_count, 1), dtype=bool), doc_ids[:, 1:] != doc_ids[:, :-1]], axis=1
    )
    doc_starts = lax.cummax(jnp.where(change, seq_index[None, :], 0), axis=1)
    key_index = jnp.arange(seq_keys, dtype=jnp.int32)
    key_inner = key_index % pair_rows
    key_place = (
        block_table[key_index // pair_rows, key_inner // half_block] * half_block
        + key_inner % half_block
    )
    key_doc = doc_ids[:, key_place]
    query_index = jnp.arange(local_rows, dtype=jnp.int32)
    query_seq = query_index // pair_rows
    query_inner = query_index % pair_rows
    query_place = (
        block_table[jnp.zeros_like(query_index) + ctx_rank, query_inner // half_block] * half_block
        + query_inner % half_block
    )
    query_doc = doc_ids[query_seq, query_place]
    query_pos = query_place - doc_starts[query_seq, query_place]
    query_place_s = query_place.reshape(seq_count, pair_rows)
    query_doc_s = query_doc.reshape(seq_count, pair_rows)
    freq_steps = jnp.arange(HD // 2, dtype=jnp.float32) * (2.0 / HD)
    angles = (
        query_pos.astype(jnp.float32)[:, None] * jnp.power(jnp.float32(THETA), -freq_steps)[None, :]
    )
    angles = jnp.concatenate([angles, angles], axis=1)[:, None, :]
    cos_table = jnp.cos(angles)
    sin_table = jnp.sin(angles)
    gain_attn, gain_query, gain_key, w_qkv, w_proj = (
        lax.all_gather(attn_gain, "ctx", axis=0, tiled=True),
        lax.all_gather(query_gain, "ctx", axis=0, tiled=True),
        lax.all_gather(key_gain, "ctx", axis=0, tiled=True),
        lax.all_gather(
            jnp.concatenate([w_query, w_key, w_value], axis=1), "ctx", axis=0, tiled=True
        ),
        lax.all_gather(w_out, "ctx", axis=1, tiled=True),
    )
    tokens_f = tokens.astype(jnp.float32)
    normal_one_f, norm_one_back = jax.vjp(normed, tokens_f, gain_attn.astype(jnp.float32))
    normal_one = normal_one_f.astype(jnp.bfloat16)
    rows_one = lax.all_gather(normal_one, "tp", axis=0, tiled=True)
    projected = jnp.dot(rows_one, w_qkv, preferred_element_type=jnp.float32)
    query_pre = projected[:, :q_width].reshape(local_rows, q_heads, HD)
    key_pre = projected[:, q_width : q_width + k_width].reshape(local_rows, kv_heads, HD)
    value_low = projected[:, q_width + k_width :].astype(jnp.bfloat16)

    def head_prep(pre_values, norm_gain):
        return rotate(normed(pre_values, norm_gain), cos_table, sin_table)

    query_rot, query_back = jax.vjp(head_prep, query_pre, gain_query.astype(jnp.float32))
    key_rot, key_back = jax.vjp(head_prep, key_pre, gain_key.astype(jnp.float32))
    query_low = query_rot.astype(jnp.bfloat16).reshape(
        seq_count, pair_rows, kv_heads, group_size, HD
    )
    key_low = key_rot.astype(jnp.bfloat16).reshape(seq_count, pair_rows, k_width)
    own_values = value_low.reshape(seq_count, pair_rows, k_width)
    keys_all, values_all = (
        lax.all_gather(key_low, "ctx", axis=1, tiled=True),
        lax.all_gather(own_values, "ctx", axis=1, tiled=True),
    )
    keys_seq = keys_all.reshape(seq_count, seq_keys, kv_heads, HD)
    values_seq = values_all.reshape(seq_count, seq_keys, kv_heads, HD)

    def tile_at(start):
        key_tile = lax.dynamic_slice_in_dim(keys_seq, start, key_block, 1)
        value_tile = lax.dynamic_slice_in_dim(values_seq, start, key_block, 1)
        place_tile = lax.dynamic_slice_in_dim(key_place, start, key_block, 0)
        doc_tile = lax.dynamic_slice_in_dim(key_doc, start, key_block, 1)
        scores = (
            jnp.einsum("sqhgd,skhd->shgqk", query_low, key_tile, preferred_element_type=jnp.float32)
            * score_scale
        )
        allowed = (doc_tile[:, None, :] == query_doc_s[:, :, None]) & (
            place_tile[None, None, :] <= query_place_s[:, :, None]
        )
        return (key_tile, value_tile, scores, allowed[:, None, None, :, :])

    starts = jnp.arange(key_blocks, dtype=jnp.int32) * key_block

    def stats_step(running, start):
        peak_score, row_total = running
        key_tile, value_tile, scores, allowed = tile_at(start)
        scores = jnp.where(allowed, scores, NEG_SCORE)
        new_peak = jnp.maximum(peak_score, jnp.max(scores, axis=-1))
        weights = jnp.where(allowed, jnp.exp(scores - new_peak[..., None]), 0.0)
        row_total = row_total * jnp.exp(peak_score - new_peak) + jnp.sum(weights, axis=-1)
        return ((new_peak, row_total), None)

    stat_shape = (seq_count, kv_heads, group_size, pair_rows)
    stats_final = lax.scan(
        stats_step,
        (jnp.full(stat_shape, NEG_SCORE, jnp.float32), jnp.zeros(stat_shape, jnp.float32)),
        starts,
    )[0]
    log_total = stats_final[0] + jnp.log(stats_final[1])

    def output_step(accum, start):
        key_tile, value_tile, scores, allowed = tile_at(start)
        probs_low = jnp.where(allowed, jnp.exp(scores - log_total[..., None]), 0.0).astype(
            jnp.bfloat16
        )
        return (
            accum
            + jnp.einsum(
                "shgqk,skhd->sqhgd", probs_low, value_tile, preferred_element_type=jnp.float32
            ),
            None,
        )

    head_shape = (seq_count, pair_rows, kv_heads, group_size, HD)
    attended = lax.scan(output_step, jnp.zeros(head_shape, jnp.float32), starts)[0]
    attn_low = attended.reshape(local_rows, q_width).astype(jnp.bfloat16)
    resid = tokens_f + lax.psum_scatter(
        jnp.dot(attn_low, w_proj, preferred_element_type=jnp.float32).astype(jnp.bfloat16),
        "tp",
        scatter_dimension=0,
        tiled=True,
    ).astype(jnp.float32)
    gain_ffn, w_gu, w_dn = (
        lax.all_gather(ffn_gain, "ctx", axis=0, tiled=True),
        lax.all_gather(jnp.concatenate([w_gate, w_up], axis=1), "ctx", axis=0, tiled=True),
        lax.all_gather(w_down, "ctx", axis=1, tiled=True),
    )
    normal_two_f, norm_two_back = jax.vjp(normed, resid, gain_ffn.astype(jnp.float32))
    normal_two = normal_two_f.astype(jnp.bfloat16)
    rows_two = lax.all_gather(normal_two, "tp", axis=0, tiled=True)
    gate_up = jnp.dot(rows_two, w_gu, preferred_element_type=jnp.float32)
    gate = gate_up[:, :ff_local]
    up_proj = gate_up[:, ff_local:]
    sigmoid_gate = jax.nn.sigmoid(gate)
    silu_gate = gate * sigmoid_gate
    hidden = (silu_gate * up_proj).astype(jnp.bfloat16)
    out = (
        resid
        + sent_and_summed(
            jnp.dot(hidden, w_dn, preferred_element_type=jnp.float32).astype(jnp.bfloat16), "tp", 0
        )
    ).astype(jnp.bfloat16)
    grad_rows = lax.all_gather(out_grad, "tp", axis=0, tiled=True)
    grad_hidden = contract_last(grad_rows, w_dn)
    grad_gate = grad_hidden * up_proj * (sigmoid_gate * (1.0 + gate * (1.0 - sigmoid_gate)))
    grad_up = grad_hidden * silu_gate
    grad_gu = jnp.concatenate([grad_gate, grad_up], axis=1).astype(jnp.bfloat16)
    mlp_grads = jnp.concatenate(
        [contract_first(rows_two, grad_gu), contract_first(grad_rows, hidden)], axis=1
    )
    mlp_early = send_grads(mlp_grads)
    grad_norm_two = sent_and_summed(contract_last(grad_gu, w_gu).astype(jnp.bfloat16), "tp", 0)
    grad_resid_norm, grad_gain_ffn = norm_two_back(grad_norm_two)
    grad_resid = out_grad.astype(jnp.float32) + grad_resid_norm
    branch_rows = lax.all_gather(grad_resid.astype(jnp.bfloat16), "tp", axis=0, tiled=True)
    grad_attn_low = contract_last(branch_rows, w_proj).astype(jnp.bfloat16)
    grad_out_cols = contract_first(branch_rows, attn_low)
    grad_attn_heads = grad_attn_low.reshape(head_shape)
    delta = jnp.transpose(
        jnp.sum(grad_attn_heads.astype(jnp.float32) * attended, axis=-1), (0, 2, 3, 1)
    )

    def scores_grad(probs, grad_probs, delta_here):
        return (probs * (grad_probs - delta_here[..., None])).astype(jnp.bfloat16)

    def grad_step(carry, start):
        accum, key_grad_all, value_grad_all = carry
        key_tile, value_tile, scores, allowed = tile_at(start)
        probs = jnp.where(allowed, jnp.exp(scores - log_total[..., None]), 0.0)
        probs_low = probs.astype(jnp.bfloat16)
        grad_value = jnp.einsum(
            "shgqk,sqhgd->skhd", probs_low, grad_attn_heads, preferred_element_type=jnp.float32
        )
        grad_probs = jnp.einsum(
            "sqhgd,skhd->shgqk", grad_attn_heads, value_tile, preferred_element_type=jnp.float32
        )
        grad_scores = scores_grad(probs, grad_probs, delta)
        accum = (
            accum
            + jnp.einsum(
                "shgqk,skhd->sqhgd", grad_scores, key_tile, preferred_element_type=jnp.float32
            )
            * score_scale
        )
        grad_key = (
            jnp.einsum(
                "shgqk,sqhgd->skhd", grad_scores, query_low, preferred_element_type=jnp.float32
            )
            * score_scale
        )
        key_grad_all = lax.dynamic_update_slice_in_dim(
            key_grad_all, grad_key.reshape(seq_count, key_block, k_width), start, 1
        )
        value_grad_all = lax.dynamic_update_slice_in_dim(
            value_grad_all, grad_value.reshape(seq_count, key_block, k_width), start, 1
        )
        return ((accum, key_grad_all, value_grad_all), None)

    kv_zero = jnp.zeros((seq_count, seq_keys, k_width), jnp.float32)
    grad_query, key_grad_all, value_grad_all = lax.scan(
        grad_step, (jnp.zeros(head_shape, jnp.float32), kv_zero, kv_zero), starts
    )[0]
    grad_keys, grad_values = (
        lax.psum_scatter(
            key_grad_all.astype(jnp.bfloat16), "ctx", scatter_dimension=1, tiled=True
        ).astype(jnp.float32),
        lax.psum_scatter(
            value_grad_all.astype(jnp.bfloat16), "ctx", scatter_dimension=1, tiled=True
        ).astype(jnp.float32),
    )
    grad_query_pre, grad_gain_query = query_back(grad_query.reshape(local_rows, q_heads, HD))
    grad_key_pre, grad_gain_key = key_back(grad_keys.reshape(local_rows, kv_heads, HD))
    grad_qkv = jnp.concatenate(
        [
            grad_query_pre.reshape(local_rows, q_width),
            grad_key_pre.reshape(local_rows, k_width),
            grad_values.reshape(local_rows, k_width),
        ],
        axis=1,
    ).astype(jnp.bfloat16)
    attn_grads = jnp.concatenate([contract_first(rows_one, grad_qkv), grad_out_cols], axis=1)
    grad_norm_one = sent_and_summed(contract_last(grad_qkv, w_qkv).astype(jnp.bfloat16), "tp", 0)
    grad_input_norm, grad_gain_attn = norm_one_back(grad_norm_one)
    grad_x = (grad_resid + grad_input_norm).astype(jnp.bfloat16)
    gain_sums = lax.psum(
        (grad_gain_attn, grad_gain_query, grad_gain_key, grad_gain_ffn), ("ctx", "tp")
    )
    d_share = gain_sums[0].shape[0] // ctx_count
    h_share = gain_sums[1].shape[0] // ctx_count
    attn_owned = send_grads(attn_grads)
    return (
        out,
        grad_x,
        lax.dynamic_slice_in_dim(gain_sums[0], ctx_rank * d_share, d_share),
        attn_owned[:, :q_width],
        attn_owned[:, q_width : q_width + k_width],
        attn_owned[:, q_width + k_width : q_width + 2 * k_width],
        lax.dynamic_slice_in_dim(gain_sums[1], ctx_rank * h_share, h_share),
        lax.dynamic_slice_in_dim(gain_sums[2], ctx_rank * h_share, h_share),
        jnp.transpose(attn_owned[:, q_width + 2 * k_width :]),
        lax.dynamic_slice_in_dim(gain_sums[3], ctx_rank * d_share, d_share),
        mlp_early[:, :ff_local],
        mlp_early[:, ff_local : 2 * ff_local],
        jnp.transpose(mlp_early[:, 2 * ff_local :]),
    )


def solution(mesh):
    in_specs = (
        P(("ctx", "tp"), None),
        P(),
        P(),
        P("ctx"),
        P("ctx", "tp"),
        P("ctx", "tp"),
        P("ctx", "tp"),
        P("ctx"),
        P("ctx"),
        P("tp", "ctx"),
        P("ctx"),
        P("ctx", "tp"),
        P("ctx", "tp"),
        P("tp", "ctx"),
        P(("ctx", "tp"), None),
    )
    out_specs = (
        P(("ctx", "tp"), None),
        P(("ctx", "tp"), None),
        P("ctx"),
        P("ctx", "tp"),
        P("ctx", "tp"),
        P("ctx", "tp"),
        P("ctx"),
        P("ctx"),
        P("tp", "ctx"),
        P("ctx"),
        P("ctx", "tp"),
        P("ctx", "tp"),
        P("tp", "ctx"),
    )
    return jax.shard_map(
        per_device, mesh=mesh, in_specs=in_specs, out_specs=out_specs, check_vma=False
    )
```

profile of v0, /device:TPU:1, one launch (start us, length us, event | category | flops | bytes accessed | tf_op | source)
XLA Modules:
  0.0 1124.1 jit_solution(7905820449707120170)
XLA Ops:
  14.7 30.3 %all-reduce.11 = (bf16[1024]{0:T(1024)(128)(2,1)S(1)}, bf16[128]{0:T(256)(128)(2,1)S(1)}, bf16[128]{0:T(256)(128)(2,1)S(1)}, bf16[1024]{0:T(1024)(128)(2,1)}) all-reduce(bf16[1024]{0:T(1024)(128)(2,1)S(1)} %dynamic-update-slice, bf16[128]{0:T(256)(128)(2,1)S(1)} %dynamic-update-slice.1, ...), channel_id=1, replica_groups=mesh['ctx'=16,'tp'=8] {'ctx'}, use_global_device_ids=true, to_apply=%add.6 | all-reduce | flops 2304 | bytes 9216
  52.0 8.8 gather_fusion.2
  60.9 9.1 gather_fusion.4
  70.9 33.8 %all-gather.9.cloned.1.call-done = bf16[1024,1024]{1,0:T(8,128)(2,1)} async-done(((bf16[128,1024]{1,0:T(8,128)(2,1)}), bf16[1024,1024]{1,0:T(8,128)(2,1)}) %all-gather.9.cloned.1.call-update) | async-done | bytes 2097168 | tf_op jit(solution)/shard_map/all_gather | solution.py:130
  104.7 3.1 fusion.161
  108.1 3.0 fusion.97
  112.1 9.1 gather_fusion.3
  124.0 33.8 %gather_fusion = s32[4096]{0:T(1024)S(1)} fusion(s32[16,2]{0,1:T(2,128)S(1)} %copy-done, s32[4096]{0:T(1024)S(1)} %bitcast.382), kind=kCustom, calls=%fused_computation | custom fusion | bytes 65536 | tf_op jit(solution)/shard_map/gather | solution.py:96
  157.9 15.8 %gather_fusion.1 = s32[4096,4]{1,0:T(8,128)} fusion(s32[4,4096]{0,1:T(8,128)} %copy.155, s32[4096]{0:T(1024)S(1)} %broadcast_clamp_fusion), kind=kCustom, calls=%fused_computation.1 | custom fusion | bytes 147456 | tf_op jit(solution)/shard_map/gather | solution.py:99
  176.6 4.9 fusion.109
  181.5 22.6 %all_gather.49 = bf16[256,1024]{0,1:T(8,128)(2,1)} all-gather(bf16[256,64]{0,1:T(8,128)(2,1)S(1)} %copy-done.40), channel_id=1, replica_groups=mesh['ctx'=16,'tp'=8] {'ctx'}, dimensions={1}, use_global_device_ids=true | all-gather | bytes 557056 | tf_op jit(solution)/shard_map/all_gather | solution.py:125
  213.8 56.3 %while.42 = (s32[]{:T(128)}, f32[4,1,2,256]{3,2,0,1:T(2,128)S(1)}, f32[4,1,2,256]{3,2,0,1:T(2,128)S(1)}, s32[8]{0:T(128)}, s32[4,4096]{1,0:T(4,128)S(1)}, /*inde...) while((s32[]{:T(128)}, f32[4,1,2,256]{3,2,0,1:T(2,128)S(1)}, ...), condition=%wide.wide.region_8.9_spmd.clone, body=%wide.wide.region_5.8_spmd.clone.sunk | while | flops 278407168 | bytes 11155674 | solution.py:179
  270.2 54.3 %while.43 = (s32[]{:T(128)}, f32[4,256,1,2,128]{1,4,3,0,2:T(8,128)S(1)}, s32[8]{0:T(128)}, bf16[4,4096,1,128]{3,1,0,2:T(8,128)(2,1)}, s32[4,4096]{1,0:T(4,128)S(...) while((s32[]{:T(128)}, ...), condition=%wide.wide.region_10.11_spmd.clone, body=%wide.wide.region_9.10_spmd.clone.sunk | while | flops 543162368 | bytes 4767452 | solution.py:200
  328.5 68.6 %reduce-scatter.10.cloned.1.call-done = bf16[128,1024]{1,0:T(8,128)(2,1)} async-done(((bf16[1024,1024]{1,0:T(8,128)(2,1)}), bf16[128,1024]{1,0:T(8,128)(2,1)}) %reduce-scatter.10.cloned.1.call-update) | async-done | bytes 262160 | tf_op jit(solution)/shard_map/reduce_scatter | solution.py:202
  400.8 23.9 %all_gather.53 = bf16[384,1024]{0,1:T(8,128)(2,1)S(1)} all-gather(bf16[384,64]{0,1:T(8,128)(2,1)} %param.34), channel_id=1, replica_groups=mesh['ctx'=16,'tp'=8] {'ctx'}, dimensions={1}, use_global_device_ids=true | all-gather | bytes 835584 | tf_op jit(solution)/shard_map/all_gather | solution.py:211
  424.7 9.1 all-gather.19.cloned.1.call-done
  433.8 55.7 %all-gather.17.cloned.1.call-done = bf16[1024,1024]{1,0:T(8,128)(2,1)} async-done(((bf16[128,1024]{1,0:T(8,128)(2,1)}), bf16[1024,1024]{1,0:T(8,128)(2,1)}) %all-gather.17.cloned.1.call-update) | async-done | bytes 2097168 | tf_op jit(solution)/shard_map/all_gather | solution.py:215
  489.5 5.5 fusion.162
  495.0 48.6 %all-gather.21.cloned.1.call-done = bf16[1024,1024]{1,0:T(8,128)(2,1)} async-done(((bf16[128,1024]{1,0:T(8,128)(2,1)}), bf16[1024,1024]{1,0:T(8,128)(2,1)}) %all-gather.21.cloned.1.call-update) | async-done | bytes 2097168 | tf_op jit(solution)/shard_map/all_gather | solution.py:228
  543.7 5.2 multiply_convert_fusion.1
  550.7 30.0 %all_to_all.15 = bf16[8,128,1024]{2,1,0:T(8,128)(2,1)S(1)} all-to-all(bf16[8,128,1024]{2,1,0:T(8,128)(2,1)S(1)} %bitcast.393), channel_id=1, replica_groups=mesh['ctx'=16,'tp'=8] {'tp'}, dimensions={0} | all-to-all | bytes 4194304 | tf_op jit(solution)/shard_map/all_to_all | solution.py:20
  583.5 52.6 %all-gather.23.cloned.1.call-done = bf16[1024,1024]{1,0:T(8,128)(2,1)} async-done(((bf16[128,1024]{1,0:T(8,128)(2,1)}), bf16[1024,1024]{1,0:T(8,128)(2,1)}) %all-gather.23.cloned.1.call-update) | async-done | bytes 2097168 | tf_op jit(solution)/shard_map/all_gather | solution.py:240
  636.1 3.1 convolution_convert_fusion.8
  648.6 176.8 %while.44 = (s32[]{:T(128)}, f32[4,256,1,2,128]{1,4,3,0,2:T(8,128)S(1)}, bf16[4,4096,128]{2,1,0:T(8,128)(2,1)}, bf16[4,4096,128]{2,1,0:T(8,128)(2,1)}, s32[8]{0:...) while((s32[]{:T(128)}, ...), condition=%wide.wide.region_18.19_spmd.clone, body=%wide.wide.region_17.18_spmd.clone.sunk | while | flops 1355546624 | bytes 29423888 | solution.py:285
  659.7 5.6 dynamic_update_slice.12
  665.3 5.6 dynamic_update_slice.13
  682.0 5.6 dynamic_update_slice.12
  687.6 5.5 dynamic_update_slice.13
  704.3 5.6 dynamic_update_slice.12
  709.8 5.6 dynamic_update_slice.13
  726.5 5.6 dynamic_update_slice.12
  732.1 5.6 dynamic_update_slice.13
  748.8 5.6 dynamic_update_slice.12
  754.4 5.5 dynamic_update_slice.13
  771.1 5.6 dynamic_update_slice.12
  776.6 5.6 dynamic_update_slice.13
  793.3 5.6 dynamic_update_slice.12
  798.9 5.6 dynamic_update_slice.13
  815.6 4.9 dynamic_update_slice.12
  820.5 4.9 dynamic_update_slice.13
  832.9 4.4 copy.197
  841.1 4.4 all-to-all-start
  854.6 41.9 %reduce-scatter.14.cloned.1.call-done = bf16[4,256,128]{2,1,0:T(8,128)(2,1)} async-done(((bf16[4,4096,128]{2,1,0:T(8,128)(2,1)}), bf16[4,256,128]{2,1,0:T(8,128)(2,1)}) %reduce-scatter.14.cloned.1.call-update) | async-done | bytes 262160 | tf_op jit(solution)/shard_map/reduce_scatter | solution.py:292
  897.6 64.9 %reduce-scatter.12.cloned.1.call-done = bf16[4,256,128]{2,1,0:T(8,128)(2,1)} async-done(((bf16[4,4096,128]{2,1,0:T(8,128)(2,1)}), bf16[4,256,128]{2,1,0:T(8,128)(2,1)}) %reduce-scatter.12.cloned.1.call-update) | async-done | bytes 262160 | tf_op jit(solution)/shard_map/reduce_scatter | solution.py:289
  972.6 3.9 convolution_convert_fusion.1
  976.5 6.8 all-to-all-start.2
  986.1 45.8 %reduce-scatter.18.cloned.1.call-done = bf16[64,1152]{1,0:T(8,128)(2,1)} async-done(((bf16[1024,1152]{1,0:T(8,128)(2,1)}), bf16[64,1152]{1,0:T(8,128)(2,1)}) %reduce-scatter.18.cloned.1.call-update) | async-done | bytes 147472
  1040.3 68.1 %all-reduce.10 = (f32[1024]{0:T(1024)S(1)}, f32[128]{0:T(128)S(1)}, f32[128]{0:T(128)S(1)}, f32[1024]{0:T(1024)S(1)}) all-reduce(f32[1024]{0:T(1024)S(1)} %get-tuple-element.576, f32[128]{0:T(128)S(1)} %get-tuple-element.574, f32[128]{0:T(128)S(1)} %get-tuple-element.570, ...), channel_id=1, replica_groups=mesh['ctx'=16,'tp'=8] {'ctx','tp'}, use_global_device_ids=true, to_apply=%region_26.27 | all-reduce | flops 2304 | bytes 18432 | tf_op jit(solution)/shard_map/psum | solution.py:310
  (477 shorter events, 254.9 us)
Async XLA Ops:
  7.2 44.9 %copy-start = (s32[16,2]{0,1:T(2,128)S(1)}, s32[16,2]{0,1:T(2,128)}, u32[]{:S(2)}) copy-start(s32[16,2]{0,1:T(2,128)} %param.22) | copy-start | bytes 388
  7.2 63.7 %all-gather.11.cloned.1.call-start = ((), (), s32[]{:S(2)}) async-start(), calls=%async_computation.9 | async-start | bytes 1114112 | tf_op jit(solution)/shard_map/all_gather | solution.py:122
  8.7 96.0 %all-gather.9.cloned.1.call-start = ((), (), s32[]{:S(2)}) async-start(), calls=%async_computation.8 | async-start | bytes 2359296 | tf_op jit(solution)/shard_map/all_gather | solution.py:130
  49.0 164.8 %all-gather.15.cloned.1.call-start = ((), (), s32[]{:S(2)}) async-start(), calls=%async_computation.11 | async-start | bytes 4456448 | tf_op jit(solution)/shard_map/all_gather | solution.py:147
  49.1 59.0 %copy-start.41 = (f32[128]{0:T(128)}, f32[128]{0:T(128)S(1)}, u32[]{:S(2)}) copy-start(f32[128]{0:T(128)S(1)} %convert_element_type.135) | copy-start | bytes 1540
  70.1 51.2 %copy-start.32 = (s32[1024]{0:T(1024)}, s32[1024]{0:T(1024)S(1)}, u32[]{:S(2)}) copy-start(s32[1024]{0:T(1024)S(1)} %get-tuple-element.1194) | copy-start | bytes 12292
  107.8 99.0 %copy-start.3 = (f32[1024,512]{0,1:T(8,128)}, f32[1024,512]{0,1:T(8,128)S(1)}, u32[]{:S(2)}) copy-start(f32[1024,512]{0,1:T(8,128)S(1)} %fusion.161) | copy-start | bytes 6291460
  107.9 3.2 copy-start.38
  108.1 4.0 copy-start.2
  112.0 158.2 %all-gather.13.cloned.1.call-start = ((), (), s32[]{:S(2)}) async-start(), calls=%async_computation.10 | async-start | bytes 4456448 | tf_op jit(solution)/shard_map/all_gather | solution.py:148
  121.2 36.6 %copy-start.34 = (s32[1024]{0:T(1024)}, s32[1024]{0:T(1024)S(1)}, u32[]{:S(2)}) copy-start(s32[1024]{0:T(1024)S(1)} %gather_fusion.3) | copy-start | bytes 12292
  157.9 23.7 %copy-start.40 = (bf16[256,64]{0,1:T(8,128)(2,1)S(1)}, bf16[256,64]{0,1:T(8,128)(2,1)}, u32[]{:S(2)}) copy-start(bf16[256,64]{0,1:T(8,128)(2,1)} %param.30) | copy-start | bytes 98308
  204.3 2.8 copy-start.6
  207.1 3.7 copy-start.14
  207.1 3.7 copy-start.22
  207.1 3.7 copy-start.23
  213.6 183.5 %reduce-scatter.10.cloned.1.call-start = ((), (), s32[]{:S(2)}) async-start(), calls=%async_computation.12 | async-start | bytes 2359296 | tf_op jit(solution)/shard_map/reduce_scatter | solution.py:202
  213.8 56.4 %copy-start.13 = (f32[4,256,1,2,128]{1,4,3,0,2:T(8,128)S(1)}, f32[4,256,1,2,128]{1,4,3,0,2:T(8,128)}, u32[]{:S(2)}) copy-start(f32[4,256,1,2,128]{1,4,3,0,2:T(8,128)} %custom-call.10) | copy-start | bytes 3145732
  325.0 2.7 copy-start.19
  325.5 2.9 copy-start.49
  325.5 71.5 %copy-start.5 = (bf16[128,1024]{1,0:T(8,128)(2,1)S(1)}, bf16[128,1024]{1,0:T(8,128)(2,1)}, u32[]{:S(2)}) copy-start(bf16[128,1024]{1,0:T(8,128)(2,1)} %param.21) | copy-start | bytes 786436
  327.7 106.2 %all-gather.19.cloned.1.call-start = ((), (), s32[]{:S(2)}) async-start(), calls=%async_computation.14 | async-start | bytes 1671168 | tf_op jit(solution)/shard_map/all_gather | solution.py:210
  328.4 161.1 %all-gather.17.cloned.1.call-start = ((), (), s32[]{:S(2)}) async-start(), calls=%async_computation.13 | async-start | bytes 2359296 | tf_op jit(solution)/shard_map/all_gather | solution.py:215
  400.0 143.7 %all-gather.21.cloned.1.call-start = ((), (), s32[]{:S(2)}) async-start(), calls=%async_computation.15 | async-start | bytes 2359296 | tf_op jit(solution)/shard_map/all_gather | solution.py:228
  400.7 235.4 %all-gather.23.cloned.1.call-start = ((), (), s32[]{:S(2)}) async-start(), calls=%async_computation.16 | async-start | bytes 2359296 | tf_op jit(solution)/shard_map/all_gather | solution.py:240
  424.7 118.9 %copy-start.24 = (bf16[384,1024]{0,1:T(8,128)(2,1)}, bf16[384,1024]{0,1:T(8,128)(2,1)S(1)}, u32[]{:S(2)}) copy-start(bf16[384,1024]{0,1:T(8,128)(2,1)S(1)} %all_gather.53) | copy-start | bytes 2359300
  543.7 5.2 copy-start.55
  582.5 56.8 %copy-start.47 = (f32[128]{0:T(128)}, f32[128]{0:T(128)S(1)}, u32[]{:S(2)}) copy-start(f32[128]{0:T(128)S(1)} %multiply_multiply_fusion.4) | copy-start | bytes 1540
  583.4 313.1 %reduce-scatter.14.cloned.1.call-start = ((), (), s32[]{:S(2)}) async-start(), calls=%async_computation.18 | async-start | bytes 4456448 | tf_op jit(solution)/shard_map/reduce_scatter | solution.py:292
  825.5 137.0 %reduce-scatter.12.cloned.1.call-start = ((), (), s32[]{:S(2)}) async-start(), calls=%async_computation.17 | async-start | bytes 4456448 | tf_op jit(solution)/shard_map/reduce_scatter | solution.py:289
  826.2 205.7 %reduce-scatter.18.cloned.1.call-start = ((), (), s32[]{:S(2)}) async-start(), calls=%async_computation.20 | async-start | bytes 2506752
  826.6 2.8 copy-start.54
  826.6 2.8 copy-start.59
  826.6 2.8 copy-start.61
  841.1 135.5 %all-to-all-start = ((bf16[8,128,1024]{2,1,0:T(8,128)(2,1)}), bf16[8,128,1024]{2,1,0:T(8,128)(2,1)}, u32[]{:S(2)}, u32[]{:S(2)}) async-start(bf16[8,128,1024]{2,1,0:T(8,128)(2,1)} %bitcast.391), calls=%async_computation.1 | async-start | bytes 4194304 | tf_op jit(solution)/shard_map/all_to_all | solution.py:20
  845.4 267.7 %reduce-scatter.16.cloned.1.call-start = ((), (), s32[]{:S(2)}) async-start(), calls=%async_computation.19 | async-start | bytes 1671168
  854.6 110.9 %copy-start.15 = (f32[1024,1,64]{0,2,1:T(8,128)S(1)}, f32[1024,1,64]{0,2,1:T(8,128)}, u32[]{:S(2)}) copy-start(f32[1024,1,64]{0,2,1:T(8,128)} %get-tuple-element.686) | copy-start | bytes 786436
  897.5 69.8 %copy-start.42 = (f32[128]{0:T(128)S(1)}, f32[128]{0:T(128)}, u32[]{:S(2)}) copy-start(f32[128]{0:T(128)} %copy-done.41) | copy-start | bytes 1540
  965.5 3.8 copy-start.39
  976.5 62.4 %all-to-all-start.2 = ((bf16[8,128,1024]{2,1,0:T(8,128)(2,1)}), bf16[8,128,1024]{2,1,0:T(8,128)(2,1)S(1)}, u32[]{:S(2)}, u32[]{:S(2)}) async-start(bf16[8,128,1024]{2,1,0:T(8,128)(2,1)} %bitcast.392), calls=%async_computation.5 | async-start | bytes 4194304 | tf_op jit(solution)/shard_map/all_to_all | solution.py:20
  1033.9 6.1 copy-start.31
  1034.0 6.1 copy-start.46
  1035.5 75.2 %copy-start.51 = (f32[128]{0:T(128)S(1)}, f32[128]{0:T(128)}, u32[]{:S(2)}) copy-start(f32[128]{0:T(128)} %copy-done.50) | copy-start | bytes 1540
  1035.5 75.2 %copy-start.9 = (f32[128,1024]{1,0:T(8,128)S(1)}, f32[128,1024]{1,0:T(8,128)}, u32[]{:S(2)}) copy-start(f32[128,1024]{1,0:T(8,128)} %copy-done.8) | copy-start | bytes 1572868
  1035.5 75.2 %copy-start.11 = (bf16[128,1024]{1,0:T(8,128)(2,1)S(1)}, bf16[128,1024]{1,0:T(8,128)(2,1)}, u32[]{:S(2)}) copy-start(bf16[128,1024]{1,0:T(8,128)(2,1)} %reduce-scatter.10.cloned.1.call-done) | copy-start | bytes 786436
  1035.5 75.3 %copy-start.17 = (bf16[128,1024]{1,0:T(8,128)(2,1)S(1)}, bf16[128,1024]{1,0:T(8,128)(2,1)}, u32[]{:S(2)}) copy-start(bf16[128,1024]{1,0:T(8,128)(2,1)} %param.35) | copy-start | bytes 786436
  1035.5 75.3 %copy-start.48 = (f32[128]{0:T(128)S(1)}, f32[128]{0:T(128)}, u32[]{:S(2)}) copy-start(f32[128]{0:T(128)} %copy-done.47) | copy-start | bytes 1540
  1110.7 6.4 copy-start.1
  (29 other events, 48.7 us)
Sparse Core Ops, SparseCore 0:
  10.3 36.2 all-gather.10
  49.5 55.1 all-gather.8
  112.1 36.1 all-gather.14
  213.7 33.6 all-gather.12
  327.8 69.2 reduce-scatter.9
  399.2 34.5 all-gather.18
  436.7 52.7 all-gather.16
  491.9 51.7 all-gather.20
  583.5 52.5 all-gather.22
  825.6 70.8 reduce-scatter.13
  898.9 63.5 reduce-scatter.11
  964.7 67.1 reduce-scatter.17
  1034.3 60.6 reduce-scatter.15
where the time goes:
time: 1140 us; the launch traced here: 1120 us
  waiting for transfers between devices  423 us (37%)
  local copies, waits for them, and re-layouts  248 us (22%)
  blocking collectives  175 us (15%)
  matrix products  135 us (12%)
  other arithmetic  66.5 us (6%)
  loops' own time  47.7 us (4%)
  between operations  16.8 us (1%)
  starting transfers between devices  12.1 us (1%)
    reduce_scatter x1, waiting for transfers between devices, per_device(): lax.psum_scatter(jnp.dot(attn_low, w_proj, preferred_element_type=jnp.flo...  68.6 us
    psum x1, blocking collectives, per_device(): lax.psum((grad_gain_attn, grad_gain_query, grad_gain_key, grad_gain_ffn),...  68.1 us
    reduce_scatter x1, waiting for transfers between devices, per_device(): lax.psum_scatter(key_grad_all.astype(jnp.bfloat16), 'ctx', scatter_dimens...  64.9 us
    all_gather x1, waiting for transfers between devices, per_device(): rows_two = lax.all_gather(normal_two, 'tp', axis=0, tiled=True)  55.7 us
    all_gather x1, waiting for transfers between devices, per_device(): lax.all_gather(grad_resid.astype(jnp.bfloat16), 'tp', axis=0, tiled=True)  52.6 us
    all_gather x1, waiting for transfers between devices, per_device(): grad_rows = lax.all_gather(out_grad, 'tp', axis=0, tiled=True)  48.6 us
    unnamed x15, waiting for transfers between devices  47.4 us
    dynamic_update_slice x8, local copies, waits for them, and re-layouts, grad_step(): lax.dynamic_update_slice_in_dim(key_grad_all, grad_key.reshape(seq_count,...  43.9 us
  transfers between devices with their start and end apart: 15, of which 9 were waited for; matrix products, arithmetic and copies ran while one was open for 18% of the time, Pallas kernels for 0%

commit v1 on v0

--- a/solution.py
+++ b/solution.py
@@ -225,7 +225,9 @@
             jnp.dot(hidden, w_dn, preferred_element_type=jnp.float32).astype(jnp.bfloat16), "tp", 0
         )
     ).astype(jnp.bfloat16)
-    grad_rows = lax.all_gather(out_grad, "tp", axis=0, tiled=True)
+    grad_rows = jnp.concatenate(
+        lax.all_to_all(jnp.stack([out_grad] * lax.axis_size("tp")), "tp", 0, 0), axis=0
+    )
     grad_hidden = contract_last(grad_rows, w_dn)
     grad_gate = grad_hidden * up_proj * (sigmoid_gate * (1.0 + gate * (1.0 - sigmoid_gate)))
     grad_up = grad_hidden * silu_gate

time: 1140 us -> 1090 us (0.956)
  waiting for transfers between devices: 423 us -> 346 us
  blocking collectives: 175 us -> 199 us
    all_gather x1 -> x0, waiting for transfers between devices: 48.6 us -> none  [per_device(): grad_rows = lax.all_gather(out_grad, 'tp', axis=0, tiled=True)]
    all_gather x1, blocking collectives: 23.9 us -> 47.5 us  [per_device(): lax.all_gather(w_down, 'ctx', axis=1, tiled=True)]
    all_gather x1, waiting for transfers between devices: 55.7 us -> 37.2 us  [per_device(): rows_two = lax.all_gather(normal_two, 'tp', axis=0, tiled=True)]
    unnamed x15 -> x14, waiting for transfers between devices: 47.4 us -> 46.7 us
  transfers between devices with their start and end apart: 15 -> 15, of which waited for: 9 -> 7; matrix products, arithmetic and copies ran while one was open for 18% -> 19% of each run, Pallas kernels for 0% -> 0%
where the time goes in v1:
time: 1090 us; the launch traced here: 1080 us
  waiting for transfers between devices  346 us (32%)
  local copies, waits for them, and re-layouts  249 us (23%)
  blocking collectives  199 us (18%)
  matrix products  135 us (12%)
  other arithmetic  66.5 us (6%)
  loops' own time  47.7 us (4%)
  between operations  17.2 us (2%)
  starting transfers between devices  16.4 us (2%)
    reduce_scatter x1, waiting for transfers between devices, per_device(): lax.psum_scatter(jnp.dot(attn_low, w_proj, preferred_element_type=jnp.flo...  68.6 us
    psum x1, blocking collectives, per_device(): lax.psum((grad_gain_attn, grad_gain_query, grad_gain_key, grad_gain_ffn),...  68.3 us
    reduce_scatter x1, waiting for transfers between devices, per_device(): lax.psum_scatter(key_grad_all.astype(jnp.bfloat16), 'ctx', scatter_dimens...  64.7 us
    all_gather x1, waiting for transfers between devices, per_device(): lax.all_gather(grad_resid.astype(jnp.bfloat16), 'tp', axis=0, tiled=True)  52.6 us
    all_gather x1, blocking collectives, per_device(): lax.all_gather(w_down, 'ctx', axis=1, tiled=True)  47.5 us
    unnamed x14, waiting for transfers between devices  46.7 us
    dynamic_update_slice x8, local copies, waits for them, and re-layouts, grad_step(): lax.dynamic_update_slice_in_dim(key_grad_all, grad_key.reshape(seq_count,...  43.8 us
    dynamic_update_slice x8, local copies, waits for them, and re-layouts, grad_step(): lax.dynamic_update_slice_in_dim(value_grad_all, grad_value.reshape(seq_co...  43.7 us
  transfers between devices with their start and end apart: 15, of which 7 were waited for; matrix products, arithmetic and copies ran while one was open for 19% of the time, Pallas kernels for 0%

profile of v1, /device:TPU:1, one launch (start us, length us, event | category | flops | bytes accessed | tf_op | source)
XLA Modules:
  0.0 1076.9 jit_solution(12098484189925053266)
XLA Ops:
  14.7 30.3 %all-reduce.11 = (bf16[1024]{0:T(1024)(128)(2,1)S(1)}, bf16[128]{0:T(256)(128)(2,1)S(1)}, bf16[128]{0:T(256)(128)(2,1)S(1)}, bf16[1024]{0:T(1024)(128)(2,1)}) all-reduce(bf16[1024]{0:T(1024)(128)(2,1)S(1)} %dynamic-update-slice, bf16[128]{0:T(256)(128)(2,1)S(1)} %dynamic-update-slice.1, ...), channel_id=1, replica_groups=mesh['ctx'=16,'tp'=8] {'ctx'}, use_global_device_ids=true, to_apply=%add.6 | all-reduce | flops 2304 | bytes 9216
  52.0 8.8 gather_fusion.2
  60.9 9.1 gather_fusion.4
  70.9 33.8 %all-gather.8.cloned.1.call-done = bf16[1024,1024]{1,0:T(8,128)(2,1)} async-done(((bf16[128,1024]{1,0:T(8,128)(2,1)}), bf16[1024,1024]{1,0:T(8,128)(2,1)}) %all-gather.8.cloned.1.call-update) | async-done | bytes 2097168 | tf_op jit(solution)/shard_map/all_gather | solution.py:130
  104.7 3.1 fusion.161
  108.1 3.1 fusion.97
  112.1 9.1 gather_fusion.3
  124.0 33.8 %gather_fusion = s32[4096]{0:T(1024)S(1)} fusion(s32[16,2]{0,1:T(2,128)S(1)} %copy-done, s32[4096]{0:T(1024)S(1)} %bitcast.383), kind=kCustom, calls=%fused_computation | custom fusion | bytes 65536 | tf_op jit(solution)/shard_map/gather | solution.py:96
  157.9 15.7 %gather_fusion.1 = s32[4096,4]{1,0:T(8,128)} fusion(s32[4,4096]{0,1:T(8,128)} %copy.155, s32[4096]{0:T(1024)S(1)} %broadcast_clamp_fusion), kind=kCustom, calls=%fused_computation.1 | custom fusion | bytes 147456 | tf_op jit(solution)/shard_map/gather | solution.py:99
  176.5 5.0 fusion.109
  181.4 22.6 %all_gather.46 = bf16[256,1024]{0,1:T(8,128)(2,1)} all-gather(bf16[256,64]{0,1:T(8,128)(2,1)S(1)} %copy-done.40), channel_id=1, replica_groups=mesh['ctx'=16,'tp'=8] {'ctx'}, dimensions={1}, use_global_device_ids=true | all-gather | bytes 557056 | tf_op jit(solution)/shard_map/all_gather | solution.py:125
  213.7 56.3 %while.42 = (s32[]{:T(128)}, f32[4,1,2,256]{3,2,0,1:T(2,128)S(1)}, f32[4,1,2,256]{3,2,0,1:T(2,128)S(1)}, s32[8]{0:T(128)}, s32[4,4096]{1,0:T(4,128)S(1)}, /*inde...) while((s32[]{:T(128)}, f32[4,1,2,256]{3,2,0,1:T(2,128)S(1)}, ...), condition=%wide.wide.region_8.9_spmd.clone, body=%wide.wide.region_5.8_spmd.clone.sunk | while | flops 278407168 | bytes 11155674 | solution.py:179
  270.0 54.3 %while.43 = (s32[]{:T(128)}, f32[4,256,1,2,128]{1,4,3,0,2:T(8,128)S(1)}, s32[8]{0:T(128)}, bf16[4,4096,1,128]{3,1,0,2:T(8,128)(2,1)}, s32[4,4096]{1,0:T(4,128)S(...) while((s32[]{:T(128)}, ...), condition=%wide.wide.region_10.11_spmd.clone, body=%wide.wide.region_9.10_spmd.clone.sunk | while | flops 543162368 | bytes 4767452 | solution.py:200
  274.0 2.8 fusion.228
  328.3 68.6 %reduce-scatter.10.cloned.1.call-done = bf16[128,1024]{1,0:T(8,128)(2,1)} async-done(((bf16[1024,1024]{1,0:T(8,128)(2,1)}), bf16[128,1024]{1,0:T(8,128)(2,1)}) %reduce-scatter.10.cloned.1.call-update) | async-done | bytes 262160 | tf_op jit(solution)/shard_map/reduce_scatter | solution.py:202
  401.6 4.4 all-to-all-start.1
  406.0 47.5 %all_gather.50 = bf16[384,1024]{0,1:T(8,128)(2,1)S(1)} all-gather(bf16[384,64]{0,1:T(8,128)(2,1)} %param.34), channel_id=1, replica_groups=mesh['ctx'=16,'tp'=8] {'ctx'}, dimensions={1}, use_global_device_ids=true | all-gather | bytes 835584 | tf_op jit(solution)/shard_map/all_gather | solution.py:211
  453.5 37.2 %all-gather.16.cloned.1.call-done = bf16[1024,1024]{1,0:T(8,128)(2,1)} async-done(((bf16[128,1024]{1,0:T(8,128)(2,1)}), bf16[1024,1024]{1,0:T(8,128)(2,1)}) %all-gather.16.cloned.1.call-update) | async-done | bytes 2097168 | tf_op jit(solution)/shard_map/all_gather | solution.py:215
  490.7 5.5 fusion.162
  496.3 5.1 multiply_convert_fusion.1
  503.3 30.0 %all_to_all.20 = bf16[8,128,1024]{2,1,0:T(8,128)(2,1)S(1)} all-to-all(bf16[8,128,1024]{2,1,0:T(8,128)(2,1)S(1)} %bitcast.394), channel_id=1, replica_groups=mesh['ctx'=16,'tp'=8] {'tp'}, dimensions={0} | all-to-all | bytes 4194304 | tf_op jit(solution)/shard_map/all_to_all | solution.py:20
  536.0 52.6 %all-gather.20.cloned.1.call-done = bf16[1024,1024]{1,0:T(8,128)(2,1)} async-done(((bf16[128,1024]{1,0:T(8,128)(2,1)}), bf16[1024,1024]{1,0:T(8,128)(2,1)}) %all-gather.20.cloned.1.call-update) | async-done | bytes 2097168 | tf_op jit(solution)/shard_map/all_gather | solution.py:242
  588.7 3.1 convolution_convert_fusion.8
  601.1 176.6 %while.44 = (s32[]{:T(128)}, f32[4,256,1,2,128]{1,4,3,0,2:T(8,128)S(1)}, bf16[4,4096,128]{2,1,0:T(8,128)(2,1)}, bf16[4,4096,128]{2,1,0:T(8,128)(2,1)}, s32[8]{0:...) while((s32[]{:T(128)}, ...), condition=%wide.wide.region_18.19_spmd.clone, body=%wide.wide.region_17.18_spmd.clone.sunk | while | flops 1355546624 | bytes 29423888 | solution.py:287
  612.3 5.6 dynamic_update_slice.12
  617.9 5.5 dynamic_update_slice.13
  634.5 5.6 dynamic_update_slice.12
  640.1 5.5 dynamic_update_slice.13
  656.8 5.6 dynamic_update_slice.12
  662.3 5.5 dynamic_update_slice.13
  679.0 5.6 dynamic_update_slice.12
  684.6 5.5 dynamic_update_slice.13
  701.2 5.6 dynamic_update_slice.12
  706.8 5.5 dynamic_update_slice.13
  723.5 5.6 dynamic_update_slice.12
  729.0 5.5 dynamic_update_slice.13
  745.7 5.6 dynamic_update_slice.12
  751.3 5.5 dynamic_update_slice.13
  767.9 4.9 dynamic_update_slice.12
  772.9 4.9 dynamic_update_slice.13
  785.2 4.3 copy.197
  793.3 4.4 all-to-all-start
  806.8 41.9 %reduce-scatter.14.cloned.1.call-done = bf16[4,256,128]{2,1,0:T(8,128)(2,1)} async-done(((bf16[4,4096,128]{2,1,0:T(8,128)(2,1)}), bf16[4,256,128]{2,1,0:T(8,128)(2,1)}) %reduce-scatter.14.cloned.1.call-update) | async-done | bytes 262160 | tf_op jit(solution)/shard_map/reduce_scatter | solution.py:294
  849.8 64.7 %reduce-scatter.12.cloned.1.call-done = bf16[4,256,128]{2,1,0:T(8,128)(2,1)} async-done(((bf16[4,4096,128]{2,1,0:T(8,128)(2,1)}), bf16[4,256,128]{2,1,0:T(8,128)(2,1)}) %reduce-scatter.12.cloned.1.call-update) | async-done | bytes 262160 | tf_op jit(solution)/shard_map/reduce_scatter | solution.py:291
  924.6 3.9 convolution_convert_fusion.1
  928.6 6.8 all-to-all-start.3
  938.1 46.0 %reduce-scatter.18.cloned.1.call-done = bf16[64,1152]{1,0:T(8,128)(2,1)} async-done(((bf16[1024,1152]{1,0:T(8,128)(2,1)}), bf16[64,1152]{1,0:T(8,128)(2,1)}) %reduce-scatter.18.cloned.1.call-update) | async-done | bytes 147472
  992.5 68.3 %all-reduce.10 = (f32[1024]{0:T(1024)S(1)}, f32[128]{0:T(128)S(1)}, f32[128]{0:T(128)S(1)}, f32[1024]{0:T(1024)S(1)}) all-reduce(f32[1024]{0:T(1024)S(1)} %get-tuple-element.576, f32[128]{0:T(128)S(1)} %get-tuple-element.574, f32[128]{0:T(128)S(1)} %get-tuple-element.570, ...), channel_id=1, replica_groups=mesh['ctx'=16,'tp'=8] {'ctx','tp'}, use_global_device_ids=true, to_apply=%region_26.27 | all-reduce | flops 2304 | bytes 18432 | tf_op jit(solution)/shard_map/psum | solution.py:312
  (477 shorter events, 252.9 us)
Async XLA Ops:
  7.2 44.8 %copy-start = (s32[16,2]{0,1:T(2,128)S(1)}, s32[16,2]{0,1:T(2,128)}, u32[]{:S(2)}) copy-start(s32[16,2]{0,1:T(2,128)} %param.22) | copy-start | bytes 388
  7.2 63.7 %all-gather.10.cloned.1.call-start = ((), (), s32[]{:S(2)}) async-start(), calls=%async_computation.10 | async-start | bytes 1114112 | tf_op jit(solution)/shard_map/all_gather | solution.py:122
  8.7 96.0 %all-gather.8.cloned.1.call-start = ((), (), s32[]{:S(2)}) async-start(), calls=%async_computation.9 | async-start | bytes 2359296 | tf_op jit(solution)/shard_map/all_gather | solution.py:130
  49.0 164.7 %all-gather.14.cloned.1.call-start = ((), (), s32[]{:S(2)}) async-start(), calls=%async_computation.12 | async-start | bytes 4456448 | tf_op jit(solution)/shard_map/all_gather | solution.py:147
  49.1 59.0 %copy-start.41 = (f32[128]{0:T(128)}, f32[128]{0:T(128)S(1)}, u32[]{:S(2)}) copy-start(f32[128]{0:T(128)S(1)} %convert_element_type.135) | copy-start | bytes 1540
  70.1 51.2 %copy-start.32 = (s32[1024]{0:T(1024)}, s32[1024]{0:T(1024)S(1)}, u32[]{:S(2)}) copy-start(s32[1024]{0:T(1024)S(1)} %get-tuple-element.1194) | copy-start | bytes 12292
  107.8 98.9 %copy-start.3 = (f32[1024,512]{0,1:T(8,128)}, f32[1024,512]{0,1:T(8,128)S(1)}, u32[]{:S(2)}) copy-start(f32[1024,512]{0,1:T(8,128)S(1)} %fusion.161) | copy-start | bytes 6291460
  107.9 3.3 copy-start.38
  108.1 4.0 copy-start.2
  112.0 158.0 %all-gather.12.cloned.1.call-start = ((), (), s32[]{:S(2)}) async-start(), calls=%async_computation.11 | async-start | bytes 4456448 | tf_op jit(solution)/shard_map/all_gather | solution.py:148
  121.3 36.6 %copy-start.34 = (s32[1024]{0:T(1024)}, s32[1024]{0:T(1024)S(1)}, u32[]{:S(2)}) copy-start(s32[1024]{0:T(1024)S(1)} %gather_fusion.3) | copy-start | bytes 12292
  157.9 23.5 %copy-start.40 = (bf16[256,64]{0,1:T(8,128)(2,1)S(1)}, bf16[256,64]{0,1:T(8,128)(2,1)}, u32[]{:S(2)}) copy-start(bf16[256,64]{0,1:T(8,128)(2,1)} %param.30) | copy-start | bytes 98308
  204.2 2.8 copy-start.6
  207.0 3.7 copy-start.14
  207.0 3.7 copy-start.22
  207.0 3.7 copy-start.23
  213.4 183.5 %reduce-scatter.10.cloned.1.call-start = ((), (), s32[]{:S(2)}) async-start(), calls=%async_computation.13 | async-start | bytes 2359296 | tf_op jit(solution)/shard_map/reduce_scatter | solution.py:202
  213.7 56.3 %copy-start.13 = (f32[4,256,1,2,128]{1,4,3,0,2:T(8,128)S(1)}, f32[4,256,1,2,128]{1,4,3,0,2:T(8,128)}, u32[]{:S(2)}) copy-start(f32[4,256,1,2,128]{1,4,3,0,2:T(8,128)} %custom-call.10) | copy-start | bytes 3145732
  325.4 2.9 copy-start.49
  325.4 71.6 %copy-start.5 = (bf16[128,1024]{1,0:T(8,128)(2,1)S(1)}, bf16[128,1024]{1,0:T(8,128)(2,1)}, u32[]{:S(2)}) copy-start(bf16[128,1024]{1,0:T(8,128)(2,1)} %param.21) | copy-start | bytes 786436
  327.5 72.4 %copy-start.16 = (bf16[128,1024]{1,0:T(8,128)(2,1)S(1)}, bf16[128,1024]{1,0:T(8,128)(2,1)}, u32[]{:S(2)}) copy-start(bf16[128,1024]{1,0:T(8,128)(2,1)} %param.35) | copy-start | bytes 786436
  327.5 126.0 %all-gather.18.cloned.1.call-start = ((), (), s32[]{:S(2)}) async-start(), calls=%async_computation.15 | async-start | bytes 1671168 | tf_op jit(solution)/shard_map/all_gather | solution.py:210
  328.3 162.5 %all-gather.16.cloned.1.call-start = ((), (), s32[]{:S(2)}) async-start(), calls=%async_computation.14 | async-start | bytes 2359296 | tf_op jit(solution)/shard_map/all_gather | solution.py:215
  401.6 94.7 %all-to-all-start.1 = ((bf16[8,128,1024]{2,1,0:T(8,128)(2,1)}), bf16[8,128,1024]{2,1,0:T(8,128)(2,1)}, u32[]{:S(2)}, u32[]{:S(2)}) async-start(bf16[8,128,1024]{2,1,0:T(8,128)(2,1)} %stack.2), calls=%async_computation.2 | async-start | bytes 4194304 | tf_op jit(solution)/shard_map/all_to_all | solution.py:229
  405.9 182.8 %all-gather.20.cloned.1.call-start = ((), (), s32[]{:S(2)}) async-start(), calls=%async_computation.16 | async-start | bytes 2359296 | tf_op jit(solution)/shard_map/all_gather | solution.py:242
  453.5 42.7 %copy-start.24 = (bf16[384,1024]{0,1:T(8,128)(2,1)}, bf16[384,1024]{0,1:T(8,128)(2,1)S(1)}, u32[]{:S(2)}) copy-start(bf16[384,1024]{0,1:T(8,128)(2,1)S(1)} %all_gather.50) | copy-start | bytes 2359300
  496.3 5.2 copy-start.55
  535.0 56.8 %copy-start.47 = (f32[128]{0:T(128)}, f32[128]{0:T(128)S(1)}, u32[]{:S(2)}) copy-start(f32[128]{0:T(128)S(1)} %multiply_multiply_fusion.4) | copy-start | bytes 1540
  535.9 312.8 %reduce-scatter.14.cloned.1.call-start = ((), (), s32[]{:S(2)}) async-start(), calls=%async_computation.18 | async-start | bytes 4456448 | tf_op jit(solution)/shard_map/reduce_scatter | solution.py:294
  777.8 136.7 %reduce-scatter.12.cloned.1.call-start = ((), (), s32[]{:S(2)}) async-start(), calls=%async_computation.17 | async-start | bytes 4456448 | tf_op jit(solution)/shard_map/reduce_scatter | solution.py:291
  778.4 205.8 %reduce-scatter.18.cloned.1.call-start = ((), (), s32[]{:S(2)}) async-start(), calls=%async_computation.20 | async-start | bytes 2506752
  779.0 2.8 copy-start.54
  779.0 2.8 copy-start.59
  779.0 2.8 copy-start.61
  793.3 135.2 %all-to-all-start = ((bf16[8,128,1024]{2,1,0:T(8,128)(2,1)}), bf16[8,128,1024]{2,1,0:T(8,128)(2,1)}, u32[]{:S(2)}, u32[]{:S(2)}) async-start(bf16[8,128,1024]{2,1,0:T(8,128)(2,1)} %bitcast.392), calls=%async_computation.1 | async-start | bytes 4194304 | tf_op jit(solution)/shard_map/all_to_all | solution.py:20
  797.7 267.9 %reduce-scatter.16.cloned.1.call-start = ((), (), s32[]{:S(2)}) async-start(), calls=%async_computation.19 | async-start | bytes 1671168
  806.8 110.7 %copy-start.15 = (f32[1024,1,64]{0,2,1:T(8,128)S(1)}, f32[1024,1,64]{0,2,1:T(8,128)}, u32[]{:S(2)}) copy-start(f32[1024,1,64]{0,2,1:T(8,128)} %get-tuple-element.686) | copy-start | bytes 786436
  849.8 69.5 %copy-start.42 = (f32[128]{0:T(128)S(1)}, f32[128]{0:T(128)}, u32[]{:S(2)}) copy-start(f32[128]{0:T(128)} %copy-done.41) | copy-start | bytes 1540
  917.5 3.8 copy-start.39
  928.6 62.6 %all-to-all-start.3 = ((bf16[8,128,1024]{2,1,0:T(8,128)(2,1)}), bf16[8,128,1024]{2,1,0:T(8,128)(2,1)S(1)}, u32[]{:S(2)}, u32[]{:S(2)}) async-start(bf16[8,128,1024]{2,1,0:T(8,128)(2,1)} %bitcast.393), calls=%async_computation.6 | async-start | bytes 4194304 | tf_op jit(solution)/shard_map/all_to_all | solution.py:20
  986.2 6.1 copy-start.31
  986.2 6.1 copy-start.46
  987.7 75.5 %copy-start.51 = (f32[128]{0:T(128)S(1)}, f32[128]{0:T(128)}, u32[]{:S(2)}) copy-start(f32[128]{0:T(128)} %copy-done.50) | copy-start | bytes 1540
  987.7 75.5 %copy-start.9 = (f32[128,1024]{1,0:T(8,128)S(1)}, f32[128,1024]{1,0:T(8,128)}, u32[]{:S(2)}) copy-start(f32[128,1024]{1,0:T(8,128)} %copy-done.8) | copy-start | bytes 1572868
  987.7 75.5 %copy-start.11 = (bf16[128,1024]{1,0:T(8,128)(2,1)S(1)}, bf16[128,1024]{1,0:T(8,128)(2,1)}, u32[]{:S(2)}) copy-start(bf16[128,1024]{1,0:T(8,128)(2,1)} %reduce-scatter.10.cloned.1.call-done) | copy-start | bytes 786436
  987.7 75.5 %copy-start.17 = (bf16[128,1024]{1,0:T(8,128)(2,1)S(1)}, bf16[128,1024]{1,0:T(8,128)(2,1)}, u32[]{:S(2)}) copy-start(bf16[128,1024]{1,0:T(8,128)(2,1)} %param.35) | copy-start | bytes 786436
  987.7 75.5 %copy-start.48 = (f32[128]{0:T(128)S(1)}, f32[128]{0:T(128)}, u32[]{:S(2)}) copy-start(f32[128]{0:T(128)} %copy-done.47) | copy-start | bytes 1540
  1063.2 6.4 copy-start.1
  (29 other events, 49.5 us)
Sparse Core Ops, SparseCore 0:
  10.3 36.2 all-gather.9
  49.5 55.1 all-gather.7
  112.2 36.1 all-gather.13
  213.5 33.6 all-gather.11
  327.6 69.2 reduce-scatter.9
  399.1 36.0 all-gather.17
  438.1 52.5 all-gather.15
  536.1 52.5 all-gather.19
  777.9 70.7 reduce-scatter.13
  851.0 63.4 reduce-scatter.11
  916.9 67.2 reduce-scatter.17
  986.4 60.6 reduce-scatter.15
